TPU v7x, 128 devices: a whole 4x4x4 slice. The times are simulated.
128 devices in a mesh: mem: 8 (over z, core), patch: 16 (over x, y).
Axes of the slice: x: 4, y: 4, z: 4, core: 2. Of those that a mesh axis runs over, the one named last changes fastest.
Arguments:
- ensemble: bfloat16 [1024, 12, 16384], P(('mem', 'patch')), may hold values from -6 to 6
- obs_col: int32 [16384], replicated, may hold values from 0 to 16383, as said below
- obs_var: int32 [16384], replicated, may hold values from 0 to 11
- obs_value: float32 [16384], replicated, may hold values from -8 to 8
- obs_err: float32 [16384], replicated, may hold values from 0.5 to 2
- obs_count: int32 [128], replicated, may hold values from 32 to 128, as said below
- coarse_list: int32 [512, 128], P(('mem', 'patch')), may hold values from 0 to 383, as said below
- coarse_count: int32 [512], P(('mem', 'patch')), may hold values from 32 to 128, as said below
Outputs:
- analysis: bfloat16 [1024, 12, 16384], P(('mem', 'patch'))
Inputs may be any that keep to these rules, and one draw needn't show every extreme that they name: `obs_col`: slot j lies in column block j // 128, so its column is between (j // 128) * 128 and that plus 128 - 1. `obs_count`: patches whose index is 0 mod 4 hold 128 observations, those 2 mod 4 hold 32, the others between 64 and 128. `coarse_list`: entries of one row are distinct window rows of the coarse point's patch, all of present observations. `coarse_count`: the first coarse point of every patch uses all 128 slots.
All inputs are finite; a program needn't handle non-finite values. Where the computation divides by a largest or mean magnitude, that divisor is 1e-20 or more.
Results may differ from a plain program's by a relative error of at most 0.0017.
Values may be sent and summed in bfloat16 or wider, within the bound.
A program may use at most 192 MiB of HBM per device.

v0:
```python
import jax
import jax.numpy as jnp
from jax import lax
from jax.sharding import PartitionSpec as P

OBS_DEV = 128
NS_STEPS = 4


def extended(array, sides, width):
    for axis, dim in sides:
        size, length = (lax.axis_size(axis), array.shape[dim])
        up = [(i, (i + 1) % size) for i in range(size)]
        down = [(j, i) for i, j in up]
        last = lax.slice_in_dim(array, length - width, length, axis=dim)
        leading = lax.slice_in_dim(array, 0, width, axis=dim)
        before = lax.ppermute(last, axis, up)
        after = lax.ppermute(leading, axis, down)
        array = jnp.concatenate([before, array, after], axis=dim)
    return array


def analyse(
    background,
    window_rows,
    values,
    errors,
    columns,
    present,
    lists,
    counts,
    first_column,
    total_columns,
):
    f32 = jnp.float32
    highest = lax.Precision.HIGHEST
    members, fields, col_count = background.shape
    blocks, slots = lists.shape
    group = col_count // blocks
    dof_ratio = members - 1.0
    wide = fields * col_count
    back_flat = background.reshape(members, wide)
    row_mean = jnp.mean(window_rows, axis=0, dtype=f32)
    obs_pert = (window_rows.astype(f32) - row_mean[None, :]).astype(jnp.bfloat16)
    innov = values - row_mean
    field_mean = jnp.mean(back_flat, axis=0, dtype=f32)
    pert_flat = (back_flat.astype(f32) - field_mean[None, :]).astype(jnp.bfloat16)
    live_slot = (jnp.arange(slots, dtype=jnp.int32)[None, :] < counts[:, None]) & present[lists]
    centre = (first_column + group * jnp.arange(blocks, dtype=jnp.int32)).astype(f32) + 0.5 * (
        group - 1
    )
    offset = columns[lists].astype(f32) - centre[:, None]
    offset = offset - total_columns * jnp.floor(offset / total_columns + 0.5)
    weight = jnp.where(live_slot, jnp.exp(-((offset / col_count) ** 2)) / errors[lists], 0.0)
    flat_list = lists.reshape(-1)
    picked = obs_pert[:, flat_list]
    full_gram = lax.dot_general(
        picked, picked, (((0,), (0,)), ((), ())), preferred_element_type=f32
    )
    block_ids = jnp.arange(blocks, dtype=jnp.int32)
    gram = full_gram.reshape(blocks, slots, blocks, slots)[block_ids, :, block_ids, :]
    identity = jnp.eye(slots, dtype=f32)
    bmat = identity + weight[:, :, None] * gram * weight[:, None, :] / dof_ratio
    scale = jnp.max(jnp.sum(jnp.abs(bmat), axis=2), axis=1)
    ymat = bmat / scale[:, None, None]
    zmat = jnp.broadcast_to(identity, bmat.shape)
    for newton_step in range(NS_STEPS):
        tmat = 0.5 * (3.0 * identity - jnp.matmul(zmat, ymat, precision=highest))
        ymat = jnp.matmul(ymat, tmat, precision=highest)
        zmat = jnp.matmul(tmat, zmat, precision=highest)
    root = jnp.sqrt(scale)[:, None, None] * ymat
    stacked = jnp.concatenate([bmat, bmat + root], axis=0)
    lowers = jnp.linalg.cholesky(stacked)
    inv_lowers = jax.scipy.linalg.solve_triangular(
        lowers, jnp.broadcast_to(identity, stacked.shape), lower=True
    )
    inv_b = inv_lowers[:blocks]
    inv_hl = inv_lowers[blocks:]
    inverse_h = jnp.matmul(jnp.swapaxes(inv_hl, 1, 2), inv_hl, precision=highest)
    rhs = weight * innov[lists]
    half = jnp.einsum("gij,gj->gi", inv_b, rhs, precision=highest)
    mean_weight = jnp.einsum("gji,gj->gi", inv_b, half, precision=highest) / dof_ratio
    mix = -(weight[:, :, None] * inverse_h * weight[:, None, :]) / dof_ratio
    shift_flat = (weight * mean_weight).reshape(-1)
    proj = lax.dot_general(picked, pert_flat, (((0,), (0,)), ((), ())), preferred_element_type=f32)
    own = (jnp.arange(blocks * slots, dtype=jnp.int32) // slots)[:, None] == (
        jnp.arange(col_count, dtype=jnp.int32) // group
    )[None, :]
    masked = jnp.where(
        own[:, None, :], proj.reshape(blocks * slots, fields, col_count), 0.0
    ).reshape(blocks * slots, wide)
    mean_term = jnp.dot(shift_flat, masked, precision=highest)
    eye_blocks = jnp.eye(blocks, dtype=f32)
    mix_full = (eye_blocks[:, None, :, None] * mix[:, :, None, :]).reshape(
        blocks * slots, blocks * slots
    )
    spread_term = lax.dot_general(
        mix_full, masked, (((0,), (0,)), ((), ())), precision=highest
    ).astype(jnp.bfloat16)
    update = jnp.dot(picked, spread_term, preferred_element_type=f32)
    total = back_flat.astype(f32) + mean_term[None, :] + update
    return total.astype(jnp.bfloat16).reshape(members, fields, col_count)


def shards(ensemble, obs_col, obs_var, obs_value, obs_err, obs_count, coarse_list, coarse_count):
    mem_count = lax.axis_size("mem")
    patch_count = lax.axis_size("patch")
    devices = mem_count * patch_count
    device_index = lax.axis_index(("mem", "patch"))
    local_members, fields, total_columns = ensemble.shape
    col_count = total_columns // devices
    background = lax.all_to_all(ensemble, ("mem", "patch"), split_axis=2, concat_axis=0, tiled=True)
    window_slot = jnp.arange(3 * OBS_DEV, dtype=jnp.int32)
    own_obs = device_index * OBS_DEV + jnp.arange(OBS_DEV, dtype=jnp.int32)
    flat_cells = obs_var[own_obs] * col_count + obs_col[own_obs] - device_index * col_count
    own_rows = background.reshape(local_members * devices, fields * col_count)[:, flat_cells]
    window_rows = extended(own_rows, ((("mem", "patch"), 1),), OBS_DEV)
    owner = (device_index - 1 + window_slot // OBS_DEV) % devices
    window_index = owner * OBS_DEV + window_slot % OBS_DEV
    present = window_slot % OBS_DEV < obs_count[owner]
    result = analyse(
        background,
        window_rows,
        obs_value[window_index],
        obs_err[window_index],
        obs_col[window_index],
        present,
        coarse_list,
        coarse_count,
        device_index * col_count,
        float(total_columns),
    )
    return lax.all_to_all(result, ("mem", "patch"), split_axis=0, concat_axis=2, tiled=True)


def solution(mesh):
    return jax.shard_map(
        shards,
        mesh=mesh,
        in_specs=(
            P(("mem", "patch"), None, None),
            P(),
            P(),
            P(),
            P(),
            P(),
            P(("mem", "patch"), None),
            P(("mem", "patch")),
        ),
        out_specs=P(("mem", "patch"), None, None),
        check_vma=False,
    )
```

profile of v0, /device:TPU:1, one launch (start us, length us, event | category | flops | bytes accessed | tf_op | source)
XLA Modules:
  0.0 569.7 jit_solution(11162033580029104701)
XLA Ops:
  0.0 27.5 %copy.100 = bf16[8,12,16384]{1,0,2:T(8,128)(2,1)} copy(bf16[8,12,16384]{2,0,1:T(8,128)(2,1)} %param.8) | data formatting | bytes 6291456 | tf_op args[0]
  27.5 63.5 %reshape.553 = bf16[128,2,6144]{2,1,0:T(2,128)(2,1)} reshape(bf16[16384,8,12]{2,1,0:T(8,128)(2,1)} %bitcast.116) | data formatting | bytes 6291456
  91.0 11.5 %all-to-all-start = ((bf16[128,2,6144]{2,1,0:T(2,128)(2,1)}), bf16[128,2,6144]{2,1,0:T(2,128)(2,1)S(1)}, u32[]{:S(2)}, u32[]{:S(2)}) async-start(bf16[128,2,6144]{2,1,0:T(2,128)(2,1)} %reshape.553), calls=%async_computation | async-start | bytes 6291456 | tf_op jit(solution)/shard_map/all_to_all | solution.py:112
  105.0 2.5 gather_fusion.2
  107.6 3.5 gather_fusion.11
  111.1 2.5 gather_fusion.4
  113.7 4.5 gather_fusion.3
  118.2 4.6 gather_fusion.5
  122.8 2.7 gather_fusion
  125.5 4.3 gather_fusion.1
  133.7 9.9 %all-to-all-done = bf16[128,2,6144]{2,1,0:T(2,128)(2,1)S(1)} async-done(((bf16[128,2,6144]{2,1,0:T(2,128)(2,1)}), bf16[128,2,6144]{2,1,0:T(2,128)(2,1)S(1)}, u32[]{:S(2)}, u32[]{:S(2)}) %all-to-all-start) | async-done | bytes 3145760 | tf_op jit(solution)/shard_map/all_to_all | solution.py:112
  143.6 78.5 %reshape.554 = bf16[16384,8,12]{2,1,0:T(8,128)(2,1)} reshape(bf16[128,2,6144]{2,1,0:T(2,128)(2,1)S(1)} %all-to-all-done) | data formatting | bytes 6291456
  222.1 29.9 %copy.101 = bf16[8,12,128,128]{3,0,1,2:T(8,128)(2,1)S(1)} copy(bf16[8,12,128,128]{1,0,3,2:T(8,128)(2,1)} %bitcast.115) | data formatting | bytes 6291456 | tf_op jit(solution)/shard_map/all_to_all | solution.py:112
  251.9 3.3 copy.103
  255.2 3.5 gather_fusion.8
  259.2 4.7 collective-permute-start.1
  264.4 2.3 fusion.3
  266.6 5.0 copy.113
  274.1 2.1 gather_fusion.9
  279.1 3.5 gather_fusion.12
  290.4 2.1 fusion.18
  292.5 95.2 %custom-call.8 = f32[8,128,128]{2,1,0:T(8,128)} custom-call(f32[8,128,128]{2,1,0:T(8,128)} %fusion.18), custom_call_target="Cholesky" | custom-call | tf_op jit(solution)/shard_map/jit(cholesky)/cholesky | solution.py:73
  391.0 80.2 %custom-call.9 = f32[8,1,128,128]{2,3,1,0:T(8,128)} custom-call(f32[8,1,128,128]{3,2,1,0:T(8,128)} %select_bitcast_fusion), custom_call_target="InvertDiagBlocksLowerTriangular" | custom-call | tf_op jit(solution)/shard_map/jit(_solve_triangular)/vmap()/triangular_solve | solution.py:74
  471.2 2.0 fusion.16
  476.5 3.1 convolution_select_fusion
  479.6 2.7 convolution_reduce_fusion
  482.6 10.2 %convolution_convert_fusion = bf16[512,1536]{1,0:T(8,128)(2,1)S(1)} fusion(f32[512,1536]{0,1:T(8,128)S(1)} %bitcast.120, f32[64,8,4,128]{3,2,1,0:T(4,128)S(1)} %bitcast.121), kind=kOutput, calls=%fused_computation.21 | convolution fusion | flops 4832624640 | bytes 5767168 | tf_op jit(solution)/shard_map/dot_general | solution.py:97
  492.8 3.5 fusion.2
  496.4 3.2 copy.117
  499.6 7.7 %copy.118 = bf16[1024,12,128]{2,1,0:T(8,128)(2,1)} copy(bf16[1024,12,128]{0,2,1:T(8,128)(2,1)S(1)} %bitcast.118) | data formatting | bytes 6291456 | tf_op jit(solution)/shard_map/reshape | solution.py:102
  507.2 59.7 %all_to_all.33 = bf16[1024,12,128]{2,1,0:T(8,128)(2,1)S(1)} all-to-all(bf16[1024,12,128]{2,1,0:T(8,128)(2,1)} %copy.118), channel_id=1, replica_groups=mesh['mem'=8,'patch'=16] {'mem','patch'}, dimensions={0} | all-to-all | bytes 6291456 | tf_op jit(solution)/shard_map/all_to_all | solution.py:133
  567.0 2.5 copy.138
  (110 shorter events, 26.9 us)
Async XLA Ops:
  0.0 103.8 %copy-start = (s32[16384]{0:T(1024)S(1)}, s32[16384]{0:T(1024)}, u32[]{:S(2)}) copy-start(s32[16384]{0:T(1024)} %param.9) | copy-start | bytes 196612
  91.0 11.6 %copy-start.7 = (s32[16384]{0:T(1024)S(1)}, s32[16384]{0:T(1024)}, u32[]{:S(2)}) copy-start(s32[16384]{0:T(1024)} %param.10) | copy-start | bytes 196612
  91.0 52.5 %all-to-all-start = ((bf16[128,2,6144]{2,1,0:T(2,128)(2,1)}), bf16[128,2,6144]{2,1,0:T(2,128)(2,1)S(1)}, u32[]{:S(2)}, u32[]{:S(2)}) async-start(bf16[128,2,6144]{2,1,0:T(2,128)(2,1)} %reshape.553), calls=%async_computation | async-start | bytes 6291456 | tf_op jit(solution)/shard_map/all_to_all | solution.py:112
  102.5 5.0 copy-start.3
  102.6 8.5 %copy-start.4 = (f32[16384]{0:T(1024)S(1)}, f32[16384]{0:T(1024)}, u32[]{:S(2)}) copy-start(f32[16384]{0:T(1024)} %param.12) | copy-start | bytes 196612
  105.0 8.7 %copy-start.16 = (s32[4,128]{1,0:T(4,128)S(1)}, s32[4,128]{1,0:T(4,128)}, u32[]{:S(2)}) copy-start(s32[4,128]{1,0:T(4,128)} %param.14) | copy-start | bytes 6148
  111.1 11.7 %copy-start.2 = (s32[128]{0:T(128)S(1)}, s32[128]{0:T(128)}, u32[]{:S(2)}) copy-start(s32[128]{0:T(128)} %param.13) | copy-start | bytes 1540
  129.8 92.2 %copy-start.13 = (f32[128,128]{1,0:T(8,128)}, f32[128,128]{1,0:T(8,128)S(1)}, u32[]{:S(2)}) copy-start(f32[128,128]{1,0:T(8,128)S(1)} %fusion.26) | copy-start | bytes 196612
  251.9 12.4 %copy-start.5 = (bf16[8,12,128,128]{3,0,1,2:T(8,128)(2,1)}, bf16[8,12,128,128]{3,0,1,2:T(8,128)(2,1)S(1)}, u32[]{:S(2)}) copy-start(bf16[8,12,128,128]{3,0,1,2:T(8,128)(2,1)S(1)} %copy.101) | copy-start | bytes 9437188
  258.7 12.9 %collective-permute-start = (bf16[1024,128]{0,1:T(8,128)(2,1)S(1)}, bf16[1024,128]{0,1:T(8,128)(2,1)}, u32[]{:S(2)}, u32[]{:S(2)}) collective-permute-start(bf16[1024,128]{0,1:T(8,128)(2,1)S(1)} %bitcast.123), channel_id=1, source_target_pairs={{0,1},{1,2},{2,3},{3,4},{4,5},{5,6},{6,7},{7,8},{8,9},{9,10},{10,1... | collective-permute-start | bytes 786440 | tf_op jit(solution)/shard_map/ppermute | solution.py:17
  259.2 12.5 %collective-permute-start.1 = (bf16[1024,128]{0,1:T(8,128)(2,1)S(1)}, bf16[1024,128]{0,1:T(8,128)(2,1)}, u32[]{:S(2)}, u32[]{:S(2)}) collective-permute-start(bf16[1024,128]{0,1:T(8,128)(2,1)S(1)} %bitcast.124), channel_id=1, source_target_pairs={{1,0},{2,1},{3,2},{4,3},{5,4},{6,5},{7,6},{8,7},{9,8},{10,9},{11,1... | collective-permute-start | bytes 786440 | tf_op jit(solution)/shard_map/ppermute | solution.py:18
  266.6 6.2 %copy-start.19 = (f32[384]{0:T(512)S(1)}, f32[384]{0:T(512)}, u32[]{:S(2)}) copy-start(f32[384]{0:T(512)} %gather_fusion.11) | copy-start | bytes 4612
  276.2 1.0 copy-start.10
  278.2 4.4 copy-start.17
  278.3 4.4 copy-start.18
  278.3 4.4 copy-start.20
  278.3 4.4 copy-start.21
  278.3 4.4 copy-start.22
  278.3 4.5 copy-start.12
  288.0 183.1 %copy-start.14 = (f32[128,128]{1,0:T(8,128)S(1)}, f32[128,128]{1,0:T(8,128)}, u32[]{:S(2)}) copy-start(f32[128,128]{1,0:T(8,128)} %copy-done.13) | copy-start | bytes 196612
  288.6 0.7 copy-start.9
  290.4 186.1 %copy-start.8 = (bf16[1536,1024]{1,0:T(8,128)(2,1)S(1)}, bf16[1536,1024]{1,0:T(8,128)(2,1)}, u32[]{:S(2)}) copy-start(bf16[1536,1024]{1,0:T(8,128)(2,1)} %copy.113) | copy-start | bytes 9437188
  290.4 186.1 %copy-start.15 = (pred[512,128]{0,1:T(8,128)(4,1)S(1)}, pred[512,128]{0,1:T(8,128)(4,1)}, u32[]{:S(2)}) copy-start(pred[512,128]{0,1:T(8,128)(4,1)} %broadcast_compare_fusion) | copy-start | bytes 196612
  482.6 10.2 %copy-start.6 = (bf16[8,12,128,128]{3,0,1,2:T(8,128)(2,1)S(1)}, bf16[8,12,128,128]{3,0,1,2:T(8,128)(2,1)}, u32[]{:S(2)}) copy-start(bf16[8,12,128,128]{3,0,1,2:T(8,128)(2,1)} %copy-done.5) | copy-start | bytes 9437188
  482.6 10.2 %copy-start.11 = (bf16[512,1024]{1,0:T(8,128)(2,1)S(1)}, bf16[512,1024]{1,0:T(8,128)(2,1)}, u32[]{:S(2)}) copy-start(bf16[512,1024]{1,0:T(8,128)(2,1)} %copy-done.10) | copy-start | bytes 3145732
  507.2 62.2 %copy-start.1 = (s32[16384]{0:T(1024)S(1)}, s32[16384]{0:T(1024)}, u32[]{:S(2)}) copy-start(s32[16384]{0:T(1024)} %param.9) | copy-start | bytes 196612
where the time goes:
time: 581 us; the launch traced here: 570 us
  local copies, waits for them, and re-layouts  263 us (45%)
  other arithmetic  190 us (33%)
  blocking collectives  59.7 us (10%)
  matrix products  30 us (5%)
  starting transfers between devices  16.6 us (3%)
  waiting for transfers between devices  9.86 us (2%)
    unnamed x49, local copies, waits for them, and re-layouts  171 us
    another operation x4, other arithmetic, analyse(): lowers = jnp.linalg.cholesky(stacked)  97.1 us
    another operation x3, other arithmetic, analyse(): jax.scipy.linalg.solve_triangular(lowers, jnp.broadcast_to(identity, stac...  82.8 us
    all_to_all x1, blocking collectives, shards(): lax.all_to_all(result, ('mem', 'patch'), split_axis=0, concat_axis=2, til...  59.7 us
    all_to_all x1, local copies, waits for them, and re-layouts, shards(): lax.all_to_all(ensemble, ('mem', 'patch'), split_axis=2, concat_axis=0, t...  29.9 us
  transfers between devices with their start and end apart: 3, of which 1 were waited for; matrix products, arithmetic and copies ran while one was open for 7% of the time, Pallas kernels for 0%

commit v1 on v0

v1 whole, which is shorter than its diff:
```python
import jax
import jax.numpy as jnp
from jax import lax
from jax.experimental import pallas as pl
from jax.experimental.pallas import tpu as pltpu
from jax.sharding import PartitionSpec as P

MESH = pl.DeviceIdType.MESH
NS_STEPS = 4
DEVICES = 128
PATCHES_Y = 16
SLOTS = 128
GROUPS = 4
GROUP_COLS = 32
COLS = 128
FIELDS = 12
LOCAL = 8
MEMBERS = 1024
WINDOW = 3 * SLOTS
STRIDE = 37
PAIR = 2
LOAD_PARTS = 4


def dot(a, b, dims, precision=None):
    return lax.dot_general(
        a, b, (dims, ((), ())), preferred_element_type=jnp.float32, precision=precision
    )


def iota(shape, dim):
    return lax.broadcasted_iota(jnp.int32, shape, dim)


def kernel(
    x_ref,
    col_ref,
    var_ref,
    value_ref,
    err_ref,
    count_ref,
    list_ref,
    list_count_ref,
    y_ref,
    xv,
    rows_out,
    rows_in,
    fields_in,
    fields_out,
    pert,
    picked,
    picked_t,
    onehot,
    weight_row,
    weight_col,
    system,
    mix3,
    shift,
    load_sem,
    rows_send,
    rows_recv,
    fields_send,
    fields_recv,
    back_send,
    back_recv,
    own_sem,
):
    f32, bf16 = jnp.float32, jnp.bfloat16
    highest = lax.Precision.HIGHEST
    mem = lax.axis_index("mem")
    patch = lax.axis_index("patch")
    me = mem * PATCHES_Y + patch
    dof = MEMBERS - 1.0

    def device(t):
        return (t >> 4, t & 15)

    def partner(i):
        return me ^ ((i * STRIDE) & (DEVICES - 1))

    def columns_of(t):
        return pl.ds(pl.multiple_of(t * COLS, COLS), COLS)

    width = DEVICES * COLS // LOAD_PARTS
    loads = []
    for part in range(LOAD_PARTS):
        span = pl.ds(part * width, width)
        load = pltpu.make_async_copy(x_ref.at[:, :, span], xv.at[:, :, span], load_sem.at[part])
        load.start()
        loads.append(load)
    barrier = pltpu.get_barrier_semaphore()

    def greet(i, carry):
        pl.semaphore_signal(barrier, inc=1, device_id=device(partner(i)), device_id_type=MESH)
        return carry

    lax.fori_loop(1, DEVICES, greet, 0)

    def extract(p, carry):
        col = col_ref[pl.ds(p, 1), :] - p * COLS
        var = var_ref[pl.ds(p, 1), :]
        hot = jnp.where(iota((COLS, SLOTS), 0) == col, 1.0, 0.0).astype(bf16)
        tile = xv[:, :, columns_of(p)].reshape(FIELDS * LOCAL, COLS)
        picks = dot(tile, hot, ((1,), (0,)))
        found = jnp.zeros((LOCAL, SLOTS), f32)
        for f in range(FIELDS):
            found = jnp.where(var == f, picks[f * LOCAL : (f + 1) * LOCAL, :], found)
        rows_out[p + 1] = found.astype(bf16)
        return carry

    share = DEVICES // LOAD_PARTS
    for part in range(LOAD_PARTS):
        loads[part].wait()
        lax.fori_loop(part * share, (part + 1) * share, extract, 0, unroll=2)
    rows_out[0] = rows_out[DEVICES]
    rows_out[DEVICES + 1] = rows_out[1]
    rows_in[:, me] = rows_out[pl.ds(me, 3)]
    fields_in[:, me] = xv[:, :, columns_of(me)]

    pl.semaphore_wait(barrier, DEVICES - 1)

    def send_rows(i, carry):
        t = partner(i)
        pltpu.make_async_remote_copy(
            src_ref=rows_out.at[pl.ds(t, 3)],
            dst_ref=rows_in.at[:, me],
            send_sem=rows_send,
            recv_sem=rows_recv,
            device_id=device(t),
            device_id_type=MESH,
        ).start()
        return carry

    lax.fori_loop(1, DEVICES, send_rows, 0)

    def send_fields(i, carry):
        t = partner(i)
        pltpu.make_async_remote_copy(
            src_ref=xv.at[:, :, columns_of(t)],
            dst_ref=fields_in.at[:, me],
            send_sem=fields_send,
            recv_sem=fields_recv,
            device_id=device(t),
            device_id_type=MESH,
        ).start()
        return carry

    lax.fori_loop(1, DEVICES, send_fields, 0)

    window = [lax.rem(me + DEVICES - 1 + w, DEVICES) for w in range(3)]
    lane = iota((1, SLOTS), 1)
    eye = iota((SLOTS, SLOTS), 0) == iota((SLOTS, SLOTS), 1)

    def window_row(ref):
        return jnp.concatenate([ref[pl.ds(q, 1), :] for q in window], axis=1)

    def as_column(row):
        return jnp.sum(jnp.where(eye, row, 0.0), axis=1, keepdims=True)

    present = jnp.concatenate(
        [jnp.where(lane < count_ref[q], 1.0, 0.0).astype(f32) for q in window], axis=1
    )
    values = window_row(value_ref)
    table = jnp.concatenate(
        [
            window_row(err_ref),
            window_row(col_ref).astype(f32),
            present,
            jnp.zeros((5, WINDOW), f32),
        ],
        axis=0,
    )
    for g in range(GROUPS):
        listed = list_ref[g : g + 1, :]
        hot = jnp.where(iota((WINDOW, SLOTS), 0) == listed, 1.0, 0.0).astype(f32)
        onehot[:, g * SLOTS : (g + 1) * SLOTS] = hot.astype(bf16)
        looked = dot(table, hot, ((1,), (0,)), highest)
        err, col, there = looked[0:1, :], looked[1:2, :], looked[2:3, :]
        centre = (me * COLS + g * GROUP_COLS).astype(f32) + 0.5 * (GROUP_COLS - 1)
        offset = col - centre
        total = float(DEVICES * COLS)
        offset = offset - total * jnp.floor(offset / total + 0.5)
        live = (lane < list_count_ref[g]) & (there > 0.5)
        weight = jnp.where(live, jnp.exp(-((offset / COLS) ** 2)) / err, 0.0)
        weight_row[g : g + 1, :] = weight
        weight_col[g] = jnp.broadcast_to(as_column(weight), (SLOTS, SLOTS))

    everyone = rows_in.at[:, pl.ds(0, DEVICES - 1)]
    pltpu.make_async_copy(everyone, everyone, rows_recv).wait()
    means = []
    for w in range(3):
        rows = rows_in[w].reshape(MEMBERS, SLOTS).astype(f32)
        mean = jnp.sum(rows, axis=0, keepdims=True) * (1.0 / MEMBERS)
        means.append(mean)
        pert[:, w * SLOTS : (w + 1) * SLOTS] = (rows - mean).astype(bf16)
    innov = values - jnp.concatenate(means, axis=1)
    innov8 = jnp.concatenate([innov, jnp.zeros((7, WINDOW), f32)], axis=0)
    for g in range(GROUPS):
        span = slice(g * SLOTS, (g + 1) * SLOTS)
        hot = onehot[:, span]
        chosen = dot(pert[...], hot, ((1,), (0,)))
        picked[:, span] = chosen.astype(bf16)
        picked_t[span, :] = jnp.transpose(chosen).astype(bf16)

    identity = jnp.where(eye, 1.0, 0.0).astype(f32)
    for g in range(GROUPS):
        span = slice(g * SLOTS, (g + 1) * SLOTS)
        gram = dot(picked_t[span, :], picked[:, span], ((1,), (0,)))
        bmat = identity + weight_col[g] * gram * weight_row[g : g + 1, :] / dof
        system[g] = bmat
    ymats, zmats, scales = [], [], []
    for g in range(GROUPS):
        bmat = system[g]
        sums = jnp.sum(jnp.abs(bmat), axis=1, keepdims=True)
        scale = jnp.max(sums, axis=0, keepdims=True)
        scales.append(scale)
        ymats.append(bmat / scale)
        zmats.append(None)
    for step in range(NS_STEPS):
        if step == 0:
            tmats = [0.5 * (3.0 * identity - y) for y in ymats]
        else:
            tmats = [
                0.5 * (3.0 * identity - dot(z, y, ((1,), (0,)), highest))
                for z, y in zip(zmats, ymats)
            ]
        ymats = [dot(y, t, ((1,), (0,)), highest) for y, t in zip(ymats, tmats)]
        if step == 0:
            zmats = tmats
        elif step < NS_STEPS - 1:
            zmats = [dot(t, z, ((1,), (0,)), highest) for t, z in zip(tmats, zmats)]
    for g in range(GROUPS):
        system[GROUPS + g] = system[g] + jnp.sqrt(scales[g]) * ymats[g]

    lanes = iota((SLOTS, SLOTS), 1)

    def sweep(k, carry):
        index = jnp.full((SLOTS, SLOTS), k, jnp.int32)
        here = lanes == k
        for j in range(2 * GROUPS):
            mat = system[j]
            row = jnp.broadcast_to(system[j, pl.ds(k, 1), :], (8, SLOTS))
            column = jnp.take_along_axis(mat, index, axis=1, mode="promise_in_bounds")
            pivot = jnp.take_along_axis(row, index[:8], axis=1, mode="promise_in_bounds")
            inverse = 1.0 / pivot
            scaled = jnp.where(here[:8], -inverse, row * inverse)
            system[j] = jnp.where(here, 0.0, mat) - column * scaled[:1]
            system[j, pl.ds(k, 1), :] = scaled[:1]
        return carry

    lax.fori_loop(0, SLOTS, sweep, 0)

    group_of = iota((SLOTS, COLS), 1) // GROUP_COLS
    shift_sel = jnp.zeros((SLOTS, COLS), f32)
    for g in range(GROUPS):
        span = slice(g * SLOTS, (g + 1) * SLOTS)
        hot = onehot[:, span].astype(f32)
        seen = dot(innov8, hot, ((1,), (0,)), highest)[0:1, :]
        row = weight_row[g : g + 1, :]
        solved = -jnp.sum(system[g] * (row * seen), axis=1, keepdims=True)
        shift_sel = jnp.where(group_of == g, weight_col[g] * solved / dof, shift_sel)
        mix = weight_col[g] * system[GROUPS + g] * row / dof
        high = mix.astype(bf16)
        low = (mix - high.astype(f32)).astype(bf16)
        mix3[span, 0:SLOTS] = high
        mix3[span, SLOTS : 2 * SLOTS] = high
        mix3[span, 2 * SLOTS : 3 * SLOTS] = low
    shift[...] = shift_sel

    everyone_in = fields_in.at[:, pl.ds(0, DEVICES - 1)]
    pltpu.make_async_copy(everyone_in, everyone_in, fields_recv).wait()

    def update(c, carry):
        first = c * PAIR
        chunk = pl.ds(first, PAIR)
        whole = [
            fields_in[first + j].reshape(MEMBERS, COLS).astype(f32) for j in range(PAIR)
        ]
        whole = jnp.concatenate(whole, axis=1)
        mean = jnp.sum(whole, axis=0, keepdims=True) * (1.0 / MEMBERS)
        field_pert = (whole - mean).astype(bf16)
        proj = dot(picked_t[...], field_pert, ((1,), (0,)))
        group = (iota((SLOTS, PAIR * COLS), 1) % COLS) // GROUP_COLS
        own = jnp.zeros((SLOTS, PAIR * COLS), f32)
        for g in range(GROUPS):
            own = jnp.where(group == g, proj[g * SLOTS : (g + 1) * SLOTS, :], own)
        both = jnp.concatenate([shift[...]] * PAIR, axis=1)
        mean_term = jnp.sum(both * own, axis=0, keepdims=True)
        high = own.astype(bf16)
        low = (own - high.astype(f32)).astype(bf16)
        split = jnp.concatenate([high, low, high], axis=0)
        spread = dot(mix3[...], split, ((1,), (0,)))
        spread = jnp.concatenate(
            [
                jnp.where(group == g, spread[g * SLOTS : (g + 1) * SLOTS, :], 0.0)
                for g in range(GROUPS)
            ],
            axis=0,
        ).astype(bf16)
        total = whole + mean_term + dot(picked[...], spread, ((1,), (0,)))
        for j in range(PAIR):
            part = total[:, j * COLS : (j + 1) * COLS].astype(bf16)
            fields_out[first + j] = part.reshape(DEVICES, LOCAL, COLS)

        def send_back(i, inner):
            t = partner(i)
            pltpu.make_async_remote_copy(
                src_ref=fields_out.at[chunk, t],
                dst_ref=y_ref.at[chunk, :, columns_of(me)],
                send_sem=back_send,
                recv_sem=back_recv,
                device_id=device(t),
                device_id_type=MESH,
            ).start()
            return inner

        lax.fori_loop(1, DEVICES, send_back, 0)
        return carry

    lax.fori_loop(0, FIELDS // PAIR, update, 0)
    mine = pltpu.make_async_copy(fields_out.at[:, me], y_ref.at[:, :, columns_of(me)], own_sem)
    mine.start()
    sent_rows = rows_in.at[:, pl.ds(0, DEVICES - 1)]
    pltpu.make_async_copy(sent_rows, sent_rows, rows_send).wait()
    pltpu.make_async_copy(everyone_in, everyone_in, fields_send).wait()
    everyone_out = fields_out.at[:, pl.ds(0, DEVICES - 1)]
    pltpu.make_async_copy(everyone_out, everyone_out, back_send).wait()
    pltpu.make_async_copy(everyone_out, everyone_out, back_recv).wait()
    mine.wait()


def shards(ensemble, obs_col, obs_var, obs_value, obs_err, obs_count, coarse_list, coarse_count):
    f32, bf16 = jnp.float32, jnp.bfloat16
    by_field = jnp.transpose(ensemble, (1, 0, 2))
    square = (DEVICES, SLOTS)
    vmem = pl.BlockSpec(memory_space=pltpu.VMEM)
    smem = pl.BlockSpec(memory_space=pltpu.SMEM)
    anywhere = pl.BlockSpec(memory_space=pl.ANY)
    blocks = (FIELDS, DEVICES, LOCAL, COLS)
    result = pl.pallas_call(
        kernel,
        out_shape=jax.ShapeDtypeStruct((FIELDS, LOCAL, DEVICES * COLS), bf16),
        in_specs=[anywhere, vmem, vmem, vmem, vmem, smem, vmem, smem],
        out_specs=anywhere,
        scratch_shapes=[
            pltpu.VMEM((FIELDS, LOCAL, DEVICES * COLS), bf16),
            pltpu.VMEM((DEVICES + 2, LOCAL, SLOTS), bf16),
            pltpu.VMEM((3, DEVICES, LOCAL, SLOTS), bf16),
            pltpu.VMEM(blocks, bf16),
            pltpu.VMEM(blocks, bf16),
            pltpu.VMEM((MEMBERS, WINDOW), bf16),
            pltpu.VMEM((MEMBERS, GROUPS * SLOTS), bf16),
            pltpu.VMEM((GROUPS * SLOTS, MEMBERS), bf16),
            pltpu.VMEM((WINDOW, GROUPS * SLOTS), bf16),
            pltpu.VMEM((8, SLOTS), f32),
            pltpu.VMEM((GROUPS, SLOTS, SLOTS), f32),
            pltpu.VMEM((2 * GROUPS, SLOTS, SLOTS), f32),
            pltpu.VMEM((GROUPS * SLOTS, 3 * SLOTS), bf16),
            pltpu.VMEM((SLOTS, COLS), f32),
            pltpu.SemaphoreType.DMA((LOAD_PARTS,)),
        ]
        + [pltpu.SemaphoreType.DMA] * 7,
        compiler_params=pltpu.CompilerParams(
            collective_id=0, has_side_effects=True, vmem_limit_bytes=48 * 1024 * 1024
        ),
        cost_estimate=pl.CostEstimate(
            flops=6_000_000_000, bytes_accessed=12_000_000, transcendentals=1024
        ),
        name="letkf",
    )(
        by_field,
        obs_col.reshape(square),
        obs_var.reshape(square),
        obs_value.reshape(square),
        obs_err.reshape(square),
        obs_count,
        coarse_list,
        coarse_count,
    )
    return jnp.transpose(result, (1, 0, 2))


def solution(mesh):
    return jax.shard_map(
        shards,
        mesh=mesh,
        in_specs=(
            P(("mem", "patch"), None, None),
            P(),
            P(),
            P(),
            P(),
            P(),
            P(("mem", "patch"), None),
            P(("mem", "patch")),
        ),
        out_specs=P(("mem", "patch"), None, None),
        check_vma=False,
    )
```

time: 581 us -> 177 us (0.30); the launches traced: 570 us -> 177 us
  local copies, waits for them, and re-layouts: 263 us -> 7.01 us
  other arithmetic: 190 us -> 0 us
  Pallas kernels: 0 us -> 170 us
  blocking collectives: 59.7 us -> 0 us
  matrix products: 30 us -> 0 us
  starting transfers between devices: 16.6 us -> 0 us
  waiting for transfers between devices: 9.86 us -> 0 us
    another operation x7 -> x0, other arithmetic: 180 us -> none  [the longest x4 97.1 us: analyse(): lowers = jnp.linalg.cholesky(stacked)]
    pallas_call x0 -> x1, Pallas kernels: none -> 170 us  [shards(): pl.pallas_call(kernel, out_shape=jax.ShapeDtypeStruct((FIELDS, LOCAL, DEV...]
    unnamed x49 -> x15, local copies, waits for them, and re-layouts: 171 us -> 7.01 us
    all_to_all x1 -> x0, blocking collectives: 59.7 us -> none  [shards(): lax.all_to_all(result, ('mem', 'patch'), split_axis=0, concat_axis=2, til...]
    gather x14 -> x0, local copies, waits for them, and re-layouts: 36.7 us -> none  [the longest x1 4.56 us: analyse(): errors[lists]]
    all_to_all x2 -> x0, local copies, waits for them, and re-layouts: 32.3 us -> none  [the longest x1 29.9 us: shards(): lax.all_to_all(ensemble, ('mem', 'patch'), split_axis=2, concat_axis=0, t...]
    dot_general x19 -> x0, matrix products: 27.9 us -> none  [the longest x1 10.2 us: analyse(): lax.dot_general(mix_full, masked, (((0,), (0,)), ((), ())), precision=hig...]
    all_to_all x1 -> x0, starting transfers between devices: 11.5 us -> none  [shards(): lax.all_to_all(ensemble, ('mem', 'patch'), split_axis=2, concat_axis=0, t...]
  transfers between devices with their start and end apart: 3 -> 0, of which waited for: 1 -> 0; matrix products, arithmetic and copies ran while one was open for 7% -> 0% of each run, Pallas kernels for 0% -> 0%
where the time goes in v1:
time: 177 us
  Pallas kernels  170 us (96%)
  local copies, waits for them, and re-layouts  7.01 us (4%)
    pallas_call x1, Pallas kernels, shards(): pl.pallas_call(kernel, out_shape=jax.ShapeDtypeStruct((FIELDS, LOCAL, DEV...  170 us
    unnamed x15, local copies, waits for them, and re-layouts  7.01 us

profile of v1, /device:TPU:1, one launch (start us, length us, event | category | flops | bytes accessed | tf_op | source)
XLA Modules:
  0.0 176.9 jit_solution(4708167662437320365)
XLA Ops:
  0.0 0.0 copy-start
  0.0 0.8 copy-done
  0.8 0.0 copy-start.1
  0.8 0.8 copy-done.1
  1.7 0.0 copy-start.2
  1.7 0.8 copy-done.2
  2.5 0.0 copy-start.3
  2.5 0.8 copy-done.3
  3.4 0.0 copy-start.4
  3.4 0.7 copy-done.4
  4.0 0.0 copy-start.5
  4.0 0.7 copy-done.5
  4.7 0.0 copy-start.6
  4.7 0.7 copy-done.6
  5.4 169.9 %letkf.1 = bf16[12,8,16384]{2,1,0:T(8,128)(2,1)S(1)} custom-call(bf16[12,8,16384]{2,1,0:T(8,128)(2,1)} %bitcast.11, s32[128,128]{1,0:T(8,128)S(1)} %bitcast.7, s32[128,128]{1,0:T(8,128)S(1)} %bitcast.8, f32[128,128]{1,0:T(8,128)S(1)} %bitcast.9, f32[128,128]{1,0:T(8,128)S(1)} %bitcast.10, s32[128]{0:T(128)S(1)} %copy-done.5, s32[4,128]{1,0:T(4,128)S(1)} %copy-done.4, ...), custom_call_target="tpu_custom_call" | custom-call | flops 6000000000 | bytes 12000000 | tf_op jit(solution)/shard_map/letkf/pallas_call | solution.py:340
  175.2 1.7 copy.10
Async XLA Ops:
  0.0 0.8 copy-start
  0.8 0.8 copy-start.1
  1.7 0.8 copy-start.2
  2.5 0.8 copy-start.3
  3.4 0.7 copy-start.4
  4.0 0.7 copy-start.5
  4.7 0.7 copy-start.6

commit v2 on v1

--- a/solution.py
+++ b/solution.py
@@ -20,6 +20,8 @@
 STRIDE = 37
 PAIR = 2
 LOAD_PARTS = 4
+EARLY = 4
+PANEL = 16
 
 
 def dot(a, b, dims, precision=None):
@@ -34,6 +36,14 @@
 
 def kernel(
     x_ref,
+    col_any,
+    var_any,
+    value_any,
+    err_any,
+    count_any,
+    list_any,
+    list_count_any,
+    y_ref,
     col_ref,
     var_ref,
     value_ref,
@@ -41,7 +51,7 @@
     count_ref,
     list_ref,
     list_count_ref,
-    y_ref,
+    small_sem,
     xv,
     rows_out,
     rows_in,
@@ -81,6 +91,21 @@
     def columns_of(t):
         return pl.ds(pl.multiple_of(t * COLS, COLS), COLS)
 
+    small = []
+    for k, (source, target) in enumerate(
+        [
+            (col_any, col_ref),
+            (var_any, var_ref),
+            (value_any, value_ref),
+            (err_any, err_ref),
+            (count_any, count_ref),
+            (list_any, list_ref),
+            (list_count_any, list_count_ref),
+        ]
+    ):
+        load = pltpu.make_async_copy(source, target, small_sem.at[k])
+        load.start()
+        small.append(load)
     width = DEVICES * COLS // LOAD_PARTS
     loads = []
     for part in range(LOAD_PARTS):
@@ -95,6 +120,29 @@
         return carry
 
     lax.fori_loop(1, DEVICES, greet, 0)
+
+    pl.semaphore_wait(barrier, DEVICES - 1)
+
+    def send_fields(first, count, part):
+        span = pl.ds(first, count)
+
+        def send(i, carry):
+            t = partner(i)
+            pltpu.make_async_remote_copy(
+                src_ref=x_ref.at[span, :, columns_of(t)],
+                dst_ref=fields_in.at[span, me],
+                send_sem=fields_send.at[part],
+                recv_sem=fields_recv.at[part],
+                device_id=device(t),
+                device_id_type=MESH,
+            ).start()
+            return carry
+
+        lax.fori_loop(1, DEVICES, send, 0)
+
+    send_fields(0, EARLY, 0)
+    for load in small:
+        load.wait()
 
     def extract(p, carry):
         col = col_ref[pl.ds(p, 1), :] - p * COLS
@@ -117,8 +165,6 @@
     rows_in[:, me] = rows_out[pl.ds(me, 3)]
     fields_in[:, me] = xv[:, :, columns_of(me)]
 
-    pl.semaphore_wait(barrier, DEVICES - 1)
-
     def send_rows(i, carry):
         t = partner(i)
         pltpu.make_async_remote_copy(
@@ -132,20 +178,7 @@
         return carry
 
     lax.fori_loop(1, DEVICES, send_rows, 0)
-
-    def send_fields(i, carry):
-        t = partner(i)
-        pltpu.make_async_remote_copy(
-            src_ref=xv.at[:, :, columns_of(t)],
-            dst_ref=fields_in.at[:, me],
-            send_sem=fields_send,
-            recv_sem=fields_recv,
-            device_id=device(t),
-            device_id_type=MESH,
-        ).start()
-        return carry
-
-    lax.fori_loop(1, DEVICES, send_fields, 0)
+    send_fields(EARLY, FIELDS - EARLY, 1)
 
     window = [lax.rem(me + DEVICES - 1 + w, DEVICES) for w in range(3)]
     lane = iota((1, SLOTS), 1)
@@ -232,23 +265,39 @@
     for g in range(GROUPS):
         system[GROUPS + g] = system[g] + jnp.sqrt(scales[g]) * ymats[g]
 
+    panel_lane = iota((1, SLOTS), 1)
+    panel_row = iota((PANEL, SLOTS), 0)
     lanes = iota((SLOTS, SLOTS), 1)
 
-    def sweep(k, carry):
-        index = jnp.full((SLOTS, SLOTS), k, jnp.int32)
-        here = lanes == k
+    def thirds(a):
+        high = a.astype(bf16)
+        rest = a - high.astype(f32)
+        mid = rest.astype(bf16)
+        return high, mid, (rest - mid.astype(f32)).astype(bf16)
+
+    for b in range(SLOTS // PANEL):
+        rows = slice(b * PANEL, (b + 1) * PANEL)
+        before = [system[j, rows, :] for j in range(2 * GROUPS)]
+        after = list(before)
+        for i in range(PANEL):
+            c = b * PANEL + i
+            here = panel_lane == c
+            for j in range(2 * GROUPS):
+                now = after[j]
+                column = jnp.broadcast_to(now[:, c : c + 1], (PANEL, SLOTS))
+                inverse = 1.0 / column[i : i + 1, :]
+                scaled = jnp.where(here, -inverse, now[i : i + 1, :] * inverse)
+                swept = jnp.where(here, 0.0, now) - column * scaled
+                after[j] = jnp.where(panel_row == i, scaled, swept)
+        inside = (lanes >= b * PANEL) & (lanes < (b + 1) * PANEL)
         for j in range(2 * GROUPS):
-            mat = system[j]
-            row = jnp.broadcast_to(system[j, pl.ds(k, 1), :], (8, SLOTS))
-            column = jnp.take_along_axis(mat, index, axis=1, mode="promise_in_bounds")
-            pivot = jnp.take_along_axis(row, index[:8], axis=1, mode="promise_in_bounds")
-            inverse = 1.0 / pivot
-            scaled = jnp.where(here[:8], -inverse, row * inverse)
-            system[j] = jnp.where(here, 0.0, mat) - column * scaled[:1]
-            system[j, pl.ds(k, 1), :] = scaled[:1]
-        return carry
-
-    lax.fori_loop(0, SLOTS, sweep, 0)
+            h, m, l = thirds(before[j])
+            p, q, r = thirds(after[j])
+            left = jnp.concatenate([h, h, h, m, m, l], axis=0)
+            right = jnp.concatenate([p, q, r, p, q, p], axis=0)
+            step = dot(left, right, ((0,), (0,)))
+            system[j] = jnp.where(inside, 0.0, system[j]) - step
+            system[j, rows, :] = after[j]
 
     group_of = iota((SLOTS, COLS), 1) // GROUP_COLS
     shift_sel = jnp.zeros((SLOTS, COLS), f32)
@@ -267,12 +316,18 @@
         mix3[span, 2 * SLOTS : 3 * SLOTS] = low
     shift[...] = shift_sel
 
-    everyone_in = fields_in.at[:, pl.ds(0, DEVICES - 1)]
-    pltpu.make_async_copy(everyone_in, everyone_in, fields_recv).wait()
+    early_in = fields_in.at[pl.ds(0, EARLY), pl.ds(0, DEVICES - 1)]
+    late_in = fields_in.at[pl.ds(EARLY, FIELDS - EARLY), pl.ds(0, DEVICES - 1)]
+    pltpu.make_async_copy(early_in, early_in, fields_recv.at[0]).wait()
 
     def update(c, carry):
         first = c * PAIR
         chunk = pl.ds(first, PAIR)
+
+        @pl.when(c == EARLY // PAIR)
+        def _():
+            pltpu.make_async_copy(late_in, late_in, fields_recv.at[1]).wait()
+
         whole = [
             fields_in[first + j].reshape(MEMBERS, COLS).astype(f32) for j in range(PAIR)
         ]
@@ -322,7 +377,8 @@
     mine.start()
     sent_rows = rows_in.at[:, pl.ds(0, DEVICES - 1)]
     pltpu.make_async_copy(sent_rows, sent_rows, rows_send).wait()
-    pltpu.make_async_copy(everyone_in, everyone_in, fields_send).wait()
+    pltpu.make_async_copy(early_in, early_in, fields_send.at[0]).wait()
+    pltpu.make_async_copy(late_in, late_in, fields_send.at[1]).wait()
     everyone_out = fields_out.at[:, pl.ds(0, DEVICES - 1)]
     pltpu.make_async_copy(everyone_out, everyone_out, back_send).wait()
     pltpu.make_async_copy(everyone_out, everyone_out, back_recv).wait()
@@ -333,16 +389,22 @@
     f32, bf16 = jnp.float32, jnp.bfloat16
     by_field = jnp.transpose(ensemble, (1, 0, 2))
     square = (DEVICES, SLOTS)
-    vmem = pl.BlockSpec(memory_space=pltpu.VMEM)
-    smem = pl.BlockSpec(memory_space=pltpu.SMEM)
     anywhere = pl.BlockSpec(memory_space=pl.ANY)
     blocks = (FIELDS, DEVICES, LOCAL, COLS)
     result = pl.pallas_call(
         kernel,
         out_shape=jax.ShapeDtypeStruct((FIELDS, LOCAL, DEVICES * COLS), bf16),
-        in_specs=[anywhere, vmem, vmem, vmem, vmem, smem, vmem, smem],
+        in_specs=[anywhere] * 8,
         out_specs=anywhere,
         scratch_shapes=[
+            pltpu.VMEM(square, jnp.int32),
+            pltpu.VMEM(square, jnp.int32),
+            pltpu.VMEM(square, f32),
+            pltpu.VMEM(square, f32),
+            pltpu.SMEM((DEVICES,), jnp.int32),
+            pltpu.VMEM((GROUPS, SLOTS), jnp.int32),
+            pltpu.SMEM((GROUPS,), jnp.int32),
+            pltpu.SemaphoreType.DMA((7,)),
             pltpu.VMEM((FIELDS, LOCAL, DEVICES * COLS), bf16),
             pltpu.VMEM((DEVICES + 2, LOCAL, SLOTS), bf16),
             pltpu.VMEM((3, DEVICES, LOCAL, SLOTS), bf16),
@@ -359,9 +421,11 @@
             pltpu.VMEM((SLOTS, COLS), f32),
             pltpu.SemaphoreType.DMA((LOAD_PARTS,)),
         ]
-        + [pltpu.SemaphoreType.DMA] * 7,
+        + [pltpu.SemaphoreType.DMA] * 2
+        + [pltpu.SemaphoreType.DMA((2,))] * 2
+        + [pltpu.SemaphoreType.DMA] * 3,
         compiler_params=pltpu.CompilerParams(
-            collective_id=0, has_side_effects=True, vmem_limit_bytes=48 * 1024 * 1024
+            collective_id=0, has_side_effects=True, vmem_limit_bytes=56 * 1024 * 1024
         ),
         cost_estimate=pl.CostEstimate(
             flops=6_000_000_000, bytes_accessed=12_000_000, transcendentals=1024

time: 177 us -> 98.9 us (0.56)
  Pallas kernels: 170 us -> 95 us
  local copies, waits for them, and re-layouts: 7.01 us -> 3.76 us
    pallas_call x1, Pallas kernels: 170 us -> 95 us  [shards(): pl.pallas_call(kernel, out_shape=jax.ShapeDtypeStruct((FIELDS, LOCAL, DEV...]
    unnamed x15 -> x1, local copies, waits for them, and re-layouts: 7.01 us -> 3.76 us
where the time goes in v2:
time: 98.9 us; the launch traced here: 98.8 us
  Pallas kernels  95 us (96%)
  local copies, waits for them, and re-layouts  3.76 us (4%)
    pallas_call x1, Pallas kernels, shards(): pl.pallas_call(kernel, out_shape=jax.ShapeDtypeStruct((FIELDS, LOCAL, DEV...  95 us
    unnamed x1, local copies, waits for them, and re-layouts  3.76 us

profile of v2, /device:TPU:1, one launch (start us, length us, event | category | flops | bytes accessed | tf_op | source)
XLA Modules:
  0.0 98.8 jit_solution(1691194171185221455)
XLA Ops:
  0.0 95.0 %letkf.1 = bf16[12,8,16384]{2,1,0:T(8,128)(2,1)} custom-call(bf16[12,8,16384]{2,1,0:T(8,128)(2,1)} %bitcast.7, s32[128,128]{1,0:T(8,128)} %bitcast.8, s32[128,128]{1,0:T(8,128)} %bitcast.9, f32[128,128]{1,0:T(8,128)} %bitcast.10, f32[128,128]{1,0:T(8,128)} %bitcast.11, s32[128]{0:T(128)} %count_any.1, s32[4,128]{1,0:T(4,128)} %list_any.1, s32[4]{0:T(128)} %list_count_any.1), custom_call_target="tpu_custom_call" | custom-call | flops 6000000000 | bytes 12000000 | tf_op jit(solution)/shard_map/letkf/pallas_call | solution.py:394
  95.0 3.8 %copy.10 = bf16[8,12,16384]{2,0,1:T(8,128)(2,1)} copy(bf16[8,12,16384]{2,0,1:T(8,128)(2,1)} %bitcast.6) | data formatting | bytes 6291456

commit v3 on v2

--- a/solution.py
+++ b/solution.py
@@ -17,10 +17,11 @@
 LOCAL = 8
 MEMBERS = 1024
 WINDOW = 3 * SLOTS
-STRIDE = 37
+STRIDE = 45
 PAIR = 2
 LOAD_PARTS = 4
 EARLY = 4
+MATES = 22
 PANEL = 16
 
 
@@ -74,6 +75,7 @@
     back_send,
     back_recv,
     own_sem,
+    ready,
 ):
     f32, bf16 = jnp.float32, jnp.bfloat16
     highest = lax.Precision.HIGHEST
@@ -115,32 +117,60 @@
         loads.append(load)
     barrier = pltpu.get_barrier_semaphore()
 
+    def mate(i):
+        return me ^ jnp.where(i < PATCHES_Y, i, (i - PATCHES_Y + 1) * PATCHES_Y)
+
     def greet(i, carry):
-        pl.semaphore_signal(barrier, inc=1, device_id=device(partner(i)), device_id_type=MESH)
+        pl.semaphore_signal(barrier, inc=1, device_id=device(mate(i)), device_id_type=MESH)
         return carry
 
-    lax.fori_loop(1, DEVICES, greet, 0)
-
-    pl.semaphore_wait(barrier, DEVICES - 1)
-
-    def send_fields(first, count, part):
-        span = pl.ds(first, count)
-
+    lax.fori_loop(1, MATES + 1, greet, 0)
+
+    def send_fields(t, part):
+        span = pl.ds(0, EARLY) if part == 0 else pl.ds(EARLY, FIELDS - EARLY)
+        pltpu.make_async_remote_copy(
+            src_ref=x_ref.at[span, :, columns_of(t)],
+            dst_ref=fields_in.at[span, me],
+            send_sem=fields_send.at[part],
+            recv_sem=fields_recv.at[part],
+            device_id=device(t),
+            device_id_type=MESH,
+        ).start()
+
+    def send_mates(part):
         def send(i, carry):
-            t = partner(i)
-            pltpu.make_async_remote_copy(
-                src_ref=x_ref.at[span, :, columns_of(t)],
-                dst_ref=fields_in.at[span, me],
-                send_sem=fields_send.at[part],
-                recv_sem=fields_recv.at[part],
-                device_id=device(t),
-                device_id_type=MESH,
-            ).start()
+            send_fields(me ^ ((i * 7) & (PATCHES_Y - 1)), part)
+
+            @pl.when(i < 8)
+            def _():
+                send_fields(me ^ (i * PATCHES_Y), part)
+
             return carry
 
+        lax.fori_loop(1, PATCHES_Y, send, 0)
+
+    def send_others(part):
+        def send(i, carry):
+            k = (i * STRIDE) & (DEVICES - 1)
+
+            @pl.when(((k & (PATCHES_Y - 1)) != 0) & (k >= PATCHES_Y))
+            def _():
+                send_fields(me ^ k, part)
+
+            return carry
+
         lax.fori_loop(1, DEVICES, send, 0)
 
-    send_fields(0, EARLY, 0)
+    pl.semaphore_wait(barrier, MATES)
+
+    def tell(i, carry):
+        pl.semaphore_signal(ready, inc=1, device_id=device(me ^ i), device_id_type=MESH)
+        return carry
+
+    lax.fori_loop(1, PATCHES_Y, tell, 0)
+    send_mates(0)
+    pl.semaphore_wait(ready, PATCHES_Y - 1)
+    send_others(0)
     for load in small:
         load.wait()
 
@@ -178,7 +208,8 @@
         return carry
 
     lax.fori_loop(1, DEVICES, send_rows, 0)
-    send_fields(EARLY, FIELDS - EARLY, 1)
+    send_mates(1)
+    send_others(1)
 
     window = [lax.rem(me + DEVICES - 1 + w, DEVICES) for w in range(3)]
     lane = iota((1, SLOTS), 1)
@@ -423,7 +454,8 @@
         ]
         + [pltpu.SemaphoreType.DMA] * 2
         + [pltpu.SemaphoreType.DMA((2,))] * 2
-        + [pltpu.SemaphoreType.DMA] * 3,
+        + [pltpu.SemaphoreType.DMA] * 3
+        + [pltpu.SemaphoreType.REGULAR],
         compiler_params=pltpu.CompilerParams(
             collective_id=0, has_side_effects=True, vmem_limit_bytes=56 * 1024 * 1024
         ),

time: 98.9 us -> 96 us (0.971)
  Pallas kernels: 95 us -> 92.1 us
    pallas_call x1, Pallas kernels: 95 us -> 92.1 us  [shards(): pl.pallas_call(kernel, out_shape=jax.ShapeDtypeStruct((FIELDS, LOCAL, DEV...]
where the time goes in v3:
time: 96 us; the launch traced here: 95.9 us
  Pallas kernels  92.1 us (96%)
  local copies, waits for them, and re-layouts  3.76 us (4%)
    pallas_call x1, Pallas kernels, shards(): pl.pallas_call(kernel, out_shape=jax.ShapeDtypeStruct((FIELDS, LOCAL, DEV...  92.1 us
    unnamed x1, local copies, waits for them, and re-layouts  3.76 us

profile of v3, /device:TPU:1, one launch (start us, length us, event | category | flops | bytes accessed | tf_op | source)
XLA Modules:
  0.0 95.9 jit_solution(9628163066025557602)
XLA Ops:
  0.0 92.1 %letkf.1 = bf16[12,8,16384]{2,1,0:T(8,128)(2,1)} custom-call(bf16[12,8,16384]{2,1,0:T(8,128)(2,1)} %bitcast.7, s32[128,128]{1,0:T(8,128)} %bitcast.8, s32[128,128]{1,0:T(8,128)} %bitcast.9, f32[128,128]{1,0:T(8,128)} %bitcast.10, f32[128,128]{1,0:T(8,128)} %bitcast.11, s32[128]{0:T(128)} %count_any.1, s32[4,128]{1,0:T(4,128)} %list_any.1, s32[4]{0:T(128)} %list_count_any.1), custom_call_target="tpu_custom_call" | custom-call | flops 6000000000 | bytes 12000000 | tf_op jit(solution)/shard_map/letkf/pallas_call | solution.py:425
  92.1 3.8 %copy.10 = bf16[8,12,16384]{2,0,1:T(8,128)(2,1)} copy(bf16[8,12,16384]{2,0,1:T(8,128)(2,1)} %bitcast.6) | data formatting | bytes 6291456

commit v4 on v3

--- a/solution.py
+++ b/solution.py
@@ -93,6 +93,17 @@
     def columns_of(t):
         return pl.ds(pl.multiple_of(t * COLS, COLS), COLS)
 
+    barrier = pltpu.get_barrier_semaphore()
+
+    def mate(i):
+        return me ^ jnp.where(i < PATCHES_Y, i, (i - PATCHES_Y + 1) * PATCHES_Y)
+
+    def greet(i, carry):
+        pl.semaphore_signal(barrier, inc=1, device_id=device(mate(i)), device_id_type=MESH)
+        return carry
+
+    lax.fori_loop(1, MATES + 1, greet, 0)
+
     small = []
     for k, (source, target) in enumerate(
         [
@@ -115,16 +126,6 @@
         load = pltpu.make_async_copy(x_ref.at[:, :, span], xv.at[:, :, span], load_sem.at[part])
         load.start()
         loads.append(load)
-    barrier = pltpu.get_barrier_semaphore()
-
-    def mate(i):
-        return me ^ jnp.where(i < PATCHES_Y, i, (i - PATCHES_Y + 1) * PATCHES_Y)
-
-    def greet(i, carry):
-        pl.semaphore_signal(barrier, inc=1, device_id=device(mate(i)), device_id_type=MESH)
-        return carry
-
-    lax.fori_loop(1, MATES + 1, greet, 0)
 
     def send_fields(t, part):
         span = pl.ds(0, EARLY) if part == 0 else pl.ds(EARLY, FIELDS - EARLY)
@@ -174,10 +175,14 @@
     for load in small:
         load.wait()
 
+    place = iota((COLS, SLOTS), 0).astype(f32).astype(bf16)
+    one, zero = jnp.ones((COLS, SLOTS), bf16), jnp.zeros((COLS, SLOTS), bf16)
+
     def extract(p, carry):
         col = col_ref[pl.ds(p, 1), :] - p * COLS
         var = var_ref[pl.ds(p, 1), :]
-        hot = jnp.where(iota((COLS, SLOTS), 0) == col, 1.0, 0.0).astype(bf16)
+        near = jnp.broadcast_to(col.astype(f32).astype(bf16), (COLS, SLOTS))
+        hot = jnp.where(place == near, one, zero)
         tile = xv[:, :, columns_of(p)].reshape(FIELDS * LOCAL, COLS)
         picks = dot(tile, hot, ((1,), (0,)))
         found = jnp.zeros((LOCAL, SLOTS), f32)
@@ -189,7 +194,7 @@
     share = DEVICES // LOAD_PARTS
     for part in range(LOAD_PARTS):
         loads[part].wait()
-        lax.fori_loop(part * share, (part + 1) * share, extract, 0, unroll=2)
+        lax.fori_loop(part * share, (part + 1) * share, extract, 0, unroll=4)
     rows_out[0] = rows_out[DEVICES]
     rows_out[DEVICES + 1] = rows_out[1]
     rows_in[:, me] = rows_out[pl.ds(me, 3)]

time: 96 us -> 95 us (0.990)
  Pallas kernels: 92.1 us -> 91.1 us
    pallas_call x1, Pallas kernels: 92.1 us -> 91.1 us  [shards(): pl.pallas_call(kernel, out_shape=jax.ShapeDtypeStruct((FIELDS, LOCAL, DEV...]
where the time goes in v4:
time: 95 us; the launch traced here: 94.8 us
  Pallas kernels  91.1 us (96%)
  local copies, waits for them, and re-layouts  3.76 us (4%)
    pallas_call x1, Pallas kernels, shards(): pl.pallas_call(kernel, out_shape=jax.ShapeDtypeStruct((FIELDS, LOCAL, DEV...  91.1 us
    unnamed x1, local copies, waits for them, and re-layouts  3.76 us

profile of v4, /device:TPU:1, one launch (start us, length us, event | category | flops | bytes accessed | tf_op | source)
XLA Modules:
  0.0 94.8 jit_solution(10326850317704389901)
XLA Ops:
  0.0 91.1 %letkf.1 = bf16[12,8,16384]{2,1,0:T(8,128)(2,1)} custom-call(bf16[12,8,16384]{2,1,0:T(8,128)(2,1)} %bitcast.7, s32[128,128]{1,0:T(8,128)} %bitcast.8, s32[128,128]{1,0:T(8,128)} %bitcast.9, f32[128,128]{1,0:T(8,128)} %bitcast.10, f32[128,128]{1,0:T(8,128)} %bitcast.11, s32[128]{0:T(128)} %count_any.1, s32[4,128]{1,0:T(4,128)} %list_any.1, s32[4]{0:T(128)} %list_count_any.1), custom_call_target="tpu_custom_call" | custom-call | flops 6000000000 | bytes 12000000 | tf_op jit(solution)/shard_map/letkf/pallas_call | solution.py:430
  91.1 3.8 %copy.10 = bf16[8,12,16384]{2,0,1:T(8,128)(2,1)} copy(bf16[8,12,16384]{2,0,1:T(8,128)(2,1)} %bitcast.6) | data formatting | bytes 6291456

commit v5 on v4

--- a/solution.py
+++ b/solution.py
@@ -393,7 +393,7 @@
             part = total[:, j * COLS : (j + 1) * COLS].astype(bf16)
             fields_out[first + j] = part.reshape(DEVICES, LOCAL, COLS)
 
-        def send_back(i, inner):
+        def send_back(i):
             t = partner(i)
             pltpu.make_async_remote_copy(
                 src_ref=fields_out.at[chunk, t],
@@ -403,9 +403,15 @@
                 device_id=device(t),
                 device_id_type=MESH,
             ).start()
+
+        def send_four(i, inner):
+            for j in range(4):
+                send_back(4 * i + j)
             return inner
 
-        lax.fori_loop(1, DEVICES, send_back, 0)
+        for i in range(1, 4):
+            send_back(i)
+        lax.fori_loop(1, DEVICES // 4, send_four, 0)
         return carry
 
     lax.fori_loop(0, FIELDS // PAIR, update, 0)

time: 95 us -> 95 us (level)
  no operation moved by 1% of the time
where the time goes in v5:
time: 95 us; the launch traced here: 94.8 us
  Pallas kernels  91.1 us (96%)
  local copies, waits for them, and re-layouts  3.76 us (4%)
    pallas_call x1, Pallas kernels, shards(): pl.pallas_call(kernel, out_shape=jax.ShapeDtypeStruct((FIELDS, LOCAL, DEV...  91.1 us
    unnamed x1, local copies, waits for them, and re-layouts  3.76 us

profile of v5, /device:TPU:1, one launch (start us, length us, event | category | flops | bytes accessed | tf_op | source)
XLA Modules:
  0.0 94.8 jit_solution(14428115551865415101)
XLA Ops:
  0.0 91.1 %letkf.1 = bf16[12,8,16384]{2,1,0:T(8,128)(2,1)} custom-call(bf16[12,8,16384]{2,1,0:T(8,128)(2,1)} %bitcast.7, s32[128,128]{1,0:T(8,128)} %bitcast.8, s32[128,128]{1,0:T(8,128)} %bitcast.9, f32[128,128]{1,0:T(8,128)} %bitcast.10, f32[128,128]{1,0:T(8,128)} %bitcast.11, s32[128]{0:T(128)} %count_any.1, s32[4,128]{1,0:T(4,128)} %list_any.1, s32[4]{0:T(128)} %list_count_any.1), custom_call_target="tpu_custom_call" | custom-call | flops 6000000000 | bytes 12000000 | tf_op jit(solution)/shard_map/letkf/pallas_call | solution.py:436
  91.1 3.8 %copy.10 = bf16[8,12,16384]{2,0,1:T(8,128)(2,1)} copy(bf16[8,12,16384]{2,0,1:T(8,128)(2,1)} %bitcast.6) | data formatting | bytes 6291456
